TPU v7x, 32 devices: a whole 2x2x4 slice. The times are simulated.
32 devices in a mesh: groups: 2 (over y), row: 4 (over x, core), col: 4 (over z).
Axes of the slice: x: 2, y: 2, z: 4, core: 2. Of those that a mesh axis runs over, the one named last changes fastest.
Arguments:
- tokens: bfloat16 [8, 4, 16, 64, 768], P(('groups', 'row'), 'col'), parts along dimension 0, may hold values from -6 to 6
- assign: int32 [8, 4, 16, 1], P(('groups', 'row'), 'col'), parts along dimension 0, may hold values from 0 to 3; in each aligned block of 16 rows (0 to 15, 16 to 31, ..., all dimensions but the last counted through in order) at most 8 rows name the same one
- level_one: float32 [8, 768, 768], P(('groups', 'row'), 'col'), parts along dimension 0, may hold values from -6 to 6
- moment_one: float32 [8, 768, 768], P(('groups', 'row'), 'col'), parts along dimension 0, may hold values from -4 to 4
- level_two: float32 [8, 768, 768], P(('groups', 'col'), 'row'), parts along dimension 0, may hold values from -6 to 6
- moment_two: float32 [8, 768, 768], P(('groups', 'col'), 'row'), parts along dimension 0, may hold values from -4 to 4
- first_one: float32 [8, 4, 768, 768], P(('groups', 'row'), 'col'), parts along dimension 0, may hold values from -0.0014648438 to 0.0014648438
- second_one: float32 [8, 4, 768, 768], P(('groups', 'row'), 'col'), parts along dimension 0, may hold values from 1e-07 to 1e-06
- first_two: float32 [8, 4, 768, 768], P(('groups', 'row'), 'col'), parts along dimension 0, may hold values from -0.0014648438 to 0.0014648438
- second_two: float32 [8, 4, 768, 768], P(('groups', 'row'), 'col'), parts along dimension 0, may hold values from 1e-07 to 1e-06
Outputs:
- level_one_new: float32 [8, 768, 768], P(('groups', 'row'), 'col'), parts along dimension 0
- moment_one_new: float32 [8, 768, 768], P(('groups', 'row'), 'col'), parts along dimension 0
- level_two_new: float32 [8, 768, 768], P(('groups', 'col'), 'row'), parts along dimension 0
- moment_two_new: float32 [8, 768, 768], P(('groups', 'col'), 'row'), parts along dimension 0
There are 2 independent parts, one for each index of `groups`. A program takes and returns all parts, laid end to end along the dimension named above; each array names one. Nothing has to cross between parts.
Inputs may be any that keep to these rules, and one draw needn't show every extreme that they name: `assign`: among the 16 blocks of one device, no level-1 module is named more than 8 times, and in some devices one is named exactly 8 times.
All inputs are finite; a program needn't handle non-finite values.
Results may differ from a plain program's by a relative error of at most 0.0012.
Values may be sent and summed in bfloat16 or wider, within the bound.
A program may use at most 128 MiB of HBM per device.

v0:
```python
import jax
import jax.numpy as jnp
from jax import lax
from jax.sharding import PartitionSpec as P

norm_eps = 1e-06
adam_eps = 1e-08
beta_first = 0.9
beta_second = 0.95
bias_first = 0.19
bias_second = 0.0975
inner_rate = 0.3
decay_rate = 0.1
outer_rate = 0.7
momentum = 0.9


def block_slots(destination, levels, capacity):
    number = destination.shape[0]
    position = jnp.arange(number, dtype=jnp.int32)
    earlier = (destination[:, None] == destination[None, :]) & (
        position[None, :] < position[:, None]
    )
    ranking = jnp.sum(earlier.astype(jnp.int32), axis=1)
    target_slot = destination * capacity + ranking
    every_slot = jnp.arange(levels * capacity, dtype=jnp.int32)
    return (every_slot[:, None] == target_slot[None, :]).astype(jnp.bfloat16)


def route_blocks(blocks, destination, levels, capacity):
    select = block_slots(destination, levels, capacity)
    number, length, features = blocks.shape
    packed = jnp.dot(
        select, blocks.reshape(number, length * features), preferred_element_type=jnp.float32
    )
    packed = packed.astype(jnp.bfloat16).reshape(levels, capacity, length, features)
    filled = jnp.sum(select, axis=1).reshape(levels, capacity)
    return (packed, filled)


def normalized(hidden):
    factor = lax.rsqrt(jnp.mean(hidden * hidden, axis=-1, keepdims=True) + norm_eps)
    return (hidden * factor, factor)


def silu_slope(preact, gating):
    return gating * (1.0 + preact * (1.0 - gating))


def path_gradients(path_slots, filled, first_weight, second_weight, loss_scale):
    number, length, features = path_slots.shape
    inputs = path_slots.astype(jnp.float32)
    targets = jnp.concatenate(
        [inputs[:, 1:], jnp.zeros((number, 1, features), jnp.float32)], axis=1
    )
    position = jnp.arange(length, dtype=jnp.int32)
    loss_weight = (
        filled.astype(jnp.float32)[:, None]
        * (position < length - 1).astype(jnp.float32)[None, :]
        * loss_scale
    )
    inputs = inputs.reshape(number * length, features)
    targets = targets.reshape(number * length, features)
    loss_weight = loss_weight.reshape(number * length, 1)
    shrink = features ** (-0.5)
    normed_one, factor_one = normalized(inputs)
    act_one = normed_one.astype(jnp.bfloat16)
    pre_one = shrink * jnp.dot(act_one, first_weight, preferred_element_type=jnp.float32)
    gate_one = jax.nn.sigmoid(pre_one)
    hidden = inputs + pre_one * gate_one
    normed_two, factor_two = normalized(hidden)
    act_two = normed_two.astype(jnp.bfloat16)
    pre_two = shrink * jnp.dot(act_two, second_weight, preferred_element_type=jnp.float32)
    gate_two = jax.nn.sigmoid(pre_two)
    output = hidden + pre_two * gate_two
    grad_out = loss_weight * (output - targets)
    grad_pre_two = (grad_out * silu_slope(pre_two, gate_two)).astype(jnp.bfloat16)
    grad_second = shrink * lax.dot_general(
        act_two, grad_pre_two, (((0,), (0,)), ((), ())), preferred_element_type=jnp.float32
    )
    grad_act_two = shrink * lax.dot_general(
        grad_pre_two, second_weight, (((1,), (1,)), ((), ())), preferred_element_type=jnp.float32
    )
    grad_hidden = grad_out + factor_two * (
        grad_act_two - normed_two * jnp.mean(grad_act_two * normed_two, axis=-1, keepdims=True)
    )
    grad_pre_one = (grad_hidden * silu_slope(pre_one, gate_one)).astype(jnp.bfloat16)
    grad_first = shrink * lax.dot_general(
        act_one, grad_pre_one, (((0,), (0,)), ((), ())), preferred_element_type=jnp.float32
    )
    return (grad_first, grad_second)


def adam_direction(gradient, first_moment, second_moment):
    first_new = beta_first * first_moment + (1.0 - beta_first) * gradient
    second_new = beta_second * second_moment + (1.0 - beta_second) * gradient * gradient
    return first_new / bias_first / (jnp.sqrt(second_new / bias_second) + adam_eps)


def outer_update(weight, moment, mean_direction):
    pseudo = inner_rate * (mean_direction + decay_rate * weight)
    moment_new = momentum * moment + pseudo
    return (weight - outer_rate * (pseudo + momentum * moment_new), moment_new)


def per_device(
    tokens,
    assign,
    level_one,
    moment_one,
    level_two,
    moment_two,
    first_one,
    second_one,
    first_two,
    second_two,
):
    levels = lax.axis_size("row")
    columns = lax.axis_size("col")
    blocks = tokens[0, 0]
    number, length, features = blocks.shape
    capacity = max(2, (2 * number + levels - 1) // levels)
    packed, filled = route_blocks(blocks, assign[0, 0, :, 0], levels, capacity)
    arrived, arrived_fill = (
        lax.all_to_all(packed, "row", split_axis=0, concat_axis=0, tiled=True),
        lax.all_to_all(filled, "row", split_axis=0, concat_axis=0, tiled=True),
    )
    first_weight = lax.all_gather(level_one.astype(jnp.bfloat16), "col", axis=1, tiled=True)[0]
    second_weight = lax.all_gather(level_two.astype(jnp.bfloat16), "row", axis=1, tiled=True)[0]
    grad_first, grad_second = path_gradients(
        arrived.reshape(levels * capacity, length, features),
        arrived_fill.reshape(levels * capacity),
        first_weight,
        second_weight,
        1.0 / (number * length),
    )
    direction_one = adam_direction(grad_first, first_one[0, 0], second_one[0, 0])
    direction_two = adam_direction(grad_second, first_two[0, 0], second_two[0, 0])
    rows_one = features // columns
    rows_two = features // levels
    total_one = lax.psum(direction_one, "col")
    total_two = lax.psum(direction_two, "row")
    mean_one = (
        lax.dynamic_slice_in_dim(total_one, lax.axis_index("col") * rows_one, rows_one, 0) / columns
    )
    mean_two = (
        lax.dynamic_slice_in_dim(total_two, lax.axis_index("row") * rows_two, rows_two, 0) / levels
    )
    new_one, new_moment_one = outer_update(level_one[0], moment_one[0], mean_one)
    new_two, new_moment_two = outer_update(level_two[0], moment_two[0], mean_two)
    return (new_one[None], new_moment_one[None], new_two[None], new_moment_two[None])


def solution(mesh):
    in_specs = (
        P(("groups", "row"), "col", None, None, None),
        P(("groups", "row"), "col", None, None),
        P(("groups", "row"), "col", None),
        P(("groups", "row"), "col", None),
        P(("groups", "col"), "row", None),
        P(("groups", "col"), "row", None),
        P(("groups", "row"), "col", None, None),
        P(("groups", "row"), "col", None, None),
        P(("groups", "row"), "col", None, None),
        P(("groups", "row"), "col", None, None),
    )
    out_specs = (
        P(("groups", "row"), "col", None),
        P(("groups", "row"), "col", None),
        P(("groups", "col"), "row", None),
        P(("groups", "col"), "row", None),
    )
    return jax.shard_map(
        per_device, mesh=mesh, in_specs=in_specs, out_specs=out_specs, check_vma=False
    )
```

profile of v0, /device:TPU:0, one launch (start us, length us, event | category | flops | bytes accessed | tf_op | source)
XLA Modules:
  0.0 278.5 jit_solution(16212694802076193530)
XLA Ops:
  7.2 0.9 convert_reduce_fusion
  9.5 4.2 %all-to-all-start.1 = ((bf16[4,1,8]{2,1,0:T(2,128)(2,1)}), bf16[4,1,8]{2,1,0:T(2,128)(2,1)S(1)}, u32[]{:S(2)}, u32[]{:S(2)}) async-start(bf16[4,1,8]{2,1,0:T(2,128)(2,1)} %all_to_all.12), calls=%async_computation.1 | async-start | bytes 4096 | tf_op jit(solution)/shard_map/all_to_all | solution.py:126
  13.7 2.3 copy.31
  16.0 1.1 convolution_convert_fusion
  17.1 2.4 copy.25
  19.4 3.7 %all-to-all-start = ((bf16[4,8,64,768]{3,2,1,0:T(8,128)(2,1)}), bf16[4,8,64,768]{3,2,1,0:T(8,128)(2,1)S(1)}, u32[]{:S(2)}, u32[]{:S(2)}) async-start(bf16[4,8,64,768]{3,2,1,0:T(8,128)(2,1)} %copy.25), calls=%async_computation | async-start | bytes 6291456 | tf_op jit(solution)/shard_map/all_to_all | solution.py:125
  23.2 1.8 convert_element_type.77
  25.1 1.8 convert_element_type.79
  27.2 32.8 %all-to-all-done = bf16[4,8,64,768]{3,2,1,0:T(8,128)(2,1)S(1)} async-done(((bf16[4,8,64,768]{3,2,1,0:T(8,128)(2,1)}), bf16[4,8,64,768]{3,2,1,0:T(8,128)(2,1)S(1)}, u32[]{:S(2)}, u32[]{:S(2)}) %all-to-all-start) | async-done | bytes 3145760 | tf_op jit(solution)/shard_map/all_to_all | solution.py:125
  60.0 0.7 multiply_reduce_fusion.2
  60.7 1.8 slice.5
  63.0 3.3 %bitcast_convert_fusion = f32[2048,768]{1,0:T(8,128)} fusion(bf16[32,64,768]{2,1,0:T(8,128)(2,1)S(1)} %concatenate.3), kind=kLoop, calls=%fused_computation.14 | loop fusion | flops 1572864 | bytes 9437184 | tf_op jit(solution)/shard_map/reshape | solution.py:63
  66.3 2.2 multiply_convert_fusion.2
  68.6 3.7 %copy.27 = f32[2048,768]{0,1:T(8,128)} copy(bf16[2048,768]{1,0:T(8,128)(2,1)S(1)} %bitcast.110) | data formatting | bytes 9437184 | tf_op jit(solution)/shard_map/convert_element_type | solution.py:52
  72.3 6.6 %copy.29 = f32[2048,768]{0,1:T(8,128)} copy(f32[2048,768]{1,0:T(8,128)} %bitcast_convert_fusion) | data formatting | bytes 12582912 | tf_op jit(solution)/shard_map/reshape | solution.py:63
  78.8 12.8 %multiply_reduce_fusion.1 = (f32[2048]{0:T(1024)S(1)}, f32[2048,768]{0,1:T(8,128)}, f32[2048,768]{0,1:T(8,128)}) fusion(f32[2048,768]{0,1:T(8,128)} %copy.27, bf16[2048,768]{1,0:T(8,128)(2,1)} %bitcast.114, bf16[1,768,768]{2,1,0:T(8,128)(2,1)} %all-gather.3.cloned.1.call-done), kind=kOutput, calls=%fused_computation.6 | convolution fusion | flops 2428499968 | bytes 23207936 | tf_op jit(solution)/shard_map/dot_general | solution.py:68
  91.7 13.3 %multiply_convert_fusion.1 = (bf16[2048,768]{0,1:T(8,128)(2,1)S(1)}, f32[2048,768]{0,1:T(8,128)}) fusion(f32[2048,768]{0,1:T(8,128)} %copy.29, f32[2048,768]{0,1:T(8,128)} %get-tuple-element.5, f32[2048]{0:T(1024)S(1)} %mul.229, bf16[1,768,768]{2,1,0:T(8,128)(2,1)} %all-gather.5.cloned.1.call-done, f32[2048]{0:T(1024)S(1)} %add_rsqrt_fusion.1), kind=kOutput, calls=%fused_computation.3 | convolution fusion | flops 2441084928 | bytes 23216128 | tf_op jit(solution)/shard_map/dot_general | solution.py:73
  105.1 4.6 %multiply_reduce_fusion = (f32[2048]{0:T(1024)S(1)}, f32[2048,768]{0,1:T(8,128)}) fusion(f32[2048,768]{0,1:T(8,128)S(1)} %copy-done, f32[2048]{0:T(1024)S(1)} %add_rsqrt_fusion.1, bf16[2048,768]{0,1:T(8,128)(2,1)S(1)} %get-tuple-element.11, bf16[1,768,768]{2,1,0:T(8,128)(2,1)S(1)} %copy-done.2), kind=kOutput, calls=%fused_computation.2 | convolution fusion | flops 2422208512 | bytes 16924672 | tf_op jit(solution)/shard_map/dot_general | solution.py:81
  109.7 5.4 %fusion.5 = f32[768,768]{1,0:T(8,128)} fusion(f32[1,1,768,768]{3,2,1,0:T(8,128)S(1)} %copy-done.4, f32[1,1,768,768]{3,2,1,0:T(8,128)S(1)} %copy-done.5, bf16[2048,768]{0,1:T(8,128)(2,1)S(1)} %get-tuple-element.11, f32[2048,768]{0,1:T(8,128)S(1)} %copy-done, f32[2048]{0:T(1024)S(1)} %add_rsqrt_fusion.1), kind=kOutput, calls=%fused_computation.20 | convolution fusion | flops 2426142720 | bytes 16523264 | tf_op jit(solution)/shard_map/dot_general | solution.py:78
  115.1 19.0 %fusion.10 = f32[768,768]{1,0:T(8,128)} fusion(f32[1,1,768,768]{3,2,1,0:T(8,128)} %param.17, f32[1,1,768,768]{3,2,1,0:T(8,128)} %param.16, f32[2048,768]{0,1:T(8,128)} %get-tuple-element.14, f32[2048,768]{0,1:T(8,128)} %get-tuple-element.10, f32[2048,768]{0,1:T(8,128)} %get-tuple-element.5, f32[2048]{0:T(1024)S(1)} %broadcast_multiply_fusion, ...), kind=kOutput, calls=%fused_computation.27 | convolution fusion | flops 2465464320 | bytes 41713664 | tf_op jit(solution)/shard_map/dot_general | solution.py:88
  134.2 37.5 %all-reduce.6.cloned.1.call-done = f32[768,768]{1,0:T(8,128)} async-done(((f32[768,768]{1,0:T(8,128)}), f32[768,768]{1,0:T(8,128)}) %all-reduce.6.cloned.1.call-update) | async-done | bytes 2359312 | tf_op jit(solution)/shard_map/psum | solution.py:142
  171.7 2.6 fusion.26
  174.3 95.3 %all-reduce.4.cloned.1.call-done = f32[768,768]{1,0:T(8,128)} async-done(((f32[768,768]{1,0:T(8,128)}), f32[768,768]{1,0:T(8,128)}) %all-reduce.4.cloned.1.call-update) | async-done | bytes 2359312 | tf_op jit(solution)/shard_map/psum | solution.py:141
  269.7 2.3 fusion.25
  (36 shorter events, 2.4 us)
Async XLA Ops:
  9.5 9.9 %all-to-all-start.1 = ((bf16[4,1,8]{2,1,0:T(2,128)(2,1)}), bf16[4,1,8]{2,1,0:T(2,128)(2,1)S(1)}, u32[]{:S(2)}, u32[]{:S(2)}) async-start(bf16[4,1,8]{2,1,0:T(2,128)(2,1)} %all_to_all.12), calls=%async_computation.1 | async-start | bytes 4096 | tf_op jit(solution)/shard_map/all_to_all | solution.py:126
  19.4 40.6 %all-to-all-start = ((bf16[4,8,64,768]{3,2,1,0:T(8,128)(2,1)}), bf16[4,8,64,768]{3,2,1,0:T(8,128)(2,1)S(1)}, u32[]{:S(2)}, u32[]{:S(2)}) async-start(bf16[4,8,64,768]{3,2,1,0:T(8,128)(2,1)} %copy.25), calls=%async_computation | async-start | bytes 6291456 | tf_op jit(solution)/shard_map/all_to_all | solution.py:125
  23.1 55.7 %all-gather.3.cloned.1.call-start = ((), (), s32[]{:S(2)}) async-start(), calls=%async_computation.2 | async-start | bytes 1474560 | tf_op jit(solution)/shard_map/all_gather | solution.py:128
  25.0 66.7 %all-gather.5.cloned.1.call-start = ((), (), s32[]{:S(2)}) async-start(), calls=%async_computation.3 | async-start | bytes 1474560 | tf_op jit(solution)/shard_map/all_gather | solution.py:129
  26.9 144.8 %all-reduce.6.cloned.1.call-start = ((), (), s32[]{:S(2)}) async-start(), calls=%async_computation.5 | async-start | bytes 4718592 | tf_op jit(solution)/shard_map/psum | solution.py:142
  91.7 13.3 %copy-start = (f32[2048,768]{0,1:T(8,128)S(1)}, f32[2048,768]{0,1:T(8,128)}, u32[]{:S(2)}) copy-start(f32[2048,768]{0,1:T(8,128)} %get-tuple-element.5) | copy-start | bytes 18874372
  91.7 13.3 %copy-start.2 = (bf16[1,768,768]{2,1,0:T(8,128)(2,1)S(1)}, bf16[1,768,768]{2,1,0:T(8,128)(2,1)}, u32[]{:S(2)}) copy-start(bf16[1,768,768]{2,1,0:T(8,128)(2,1)} %all-gather.5.cloned.1.call-done) | copy-start | bytes 3538948
  105.0 4.6 %copy-start.4 = (f32[1,1,768,768]{3,2,1,0:T(8,128)S(1)}, f32[1,1,768,768]{3,2,1,0:T(8,128)}, u32[]{:S(2)}) copy-start(f32[1,1,768,768]{3,2,1,0:T(8,128)} %param.19) | copy-start | bytes 7077892
  105.0 4.6 %copy-start.5 = (f32[1,1,768,768]{3,2,1,0:T(8,128)S(1)}, f32[1,1,768,768]{3,2,1,0:T(8,128)}, u32[]{:S(2)}) copy-start(f32[1,1,768,768]{3,2,1,0:T(8,128)} %param.18) | copy-start | bytes 7077892
  115.1 154.6 %all-reduce.4.cloned.1.call-start = ((), (), s32[]{:S(2)}) async-start(), calls=%async_computation.4 | async-start | bytes 4718592 | tf_op jit(solution)/shard_map/psum | solution.py:141
  134.2 135.5 %copy-start.1 = (f32[1,192,768]{2,1,0:T(8,128)S(1)}, f32[1,192,768]{2,1,0:T(8,128)}, u32[]{:S(2)}) copy-start(f32[1,192,768]{2,1,0:T(8,128)} %param.12) | copy-start | bytes 1769476
  134.2 135.5 %copy-start.3 = (f32[1,192,768]{2,1,0:T(8,128)S(1)}, f32[1,192,768]{2,1,0:T(8,128)}, u32[]{:S(2)}) copy-start(f32[1,192,768]{2,1,0:T(8,128)} %param.13) | copy-start | bytes 1769476
Sparse Core Ops, SparseCore 0:
  26.1 32.6 all-gather.2
  60.9 16.5 all-gather.4
  115.2 56.4 all-reduce.5
  173.9 95.7 all-reduce.3
where the time goes:
time: 279 us; the launch traced here: 278 us
  waiting for transfers between devices  166 us (59%)
  matrix products  56.3 us (20%)
  local copies, waits for them, and re-layouts  18 us (6%)
  other arithmetic  16.6 us (6%)
  between operations  13.9 us (5%)
  starting transfers between devices  8.07 us (3%)
    psum x1, waiting for transfers between devices, per_device(): total_one = lax.psum(direction_one, 'col')  95.3 us
    psum x1, waiting for transfers between devices, per_device(): total_two = lax.psum(direction_two, 'row')  37.5 us
    all_to_all x1, waiting for transfers between devices, per_device(): lax.all_to_all(packed, 'row', split_axis=0, concat_axis=0, tiled=True)  32.8 us
    dot_general x1, matrix products, path_gradients(): lax.dot_general(act_one, grad_pre_one, (((0,), (0,)), ((), ())), preferre...  19 us
    dot_general x1, matrix products, path_gradients(): jnp.dot(act_two, second_weight, preferred_element_type=jnp.float32)  13.3 us
    dot_general x1, matrix products, path_gradients(): jnp.dot(act_one, first_weight, preferred_element_type=jnp.float32)  12.8 us
    reshape x1, local copies, waits for them, and re-layouts, path_gradients(): targets = targets.reshape(number * length, features)  6.57 us
  transfers between devices with their start and end apart: 6, of which 3 were waited for; matrix products, arithmetic and copies ran while one was open for 23% of the time, Pallas kernels for 0%

commit v1 on v0

v1 whole, which is shorter than its diff:
```python
import functools

import jax
import jax.numpy as jnp
from jax import lax
from jax.experimental import pallas as pl
from jax.experimental.pallas import tpu as pltpu
from jax.sharding import PartitionSpec as P

norm_eps = 1e-06
adam_eps = 1e-08
beta_first = 0.9
beta_second = 0.95
bias_first = 0.19
bias_second = 0.0975
inner_rate = 0.3
decay_rate = 0.1
outer_rate = 0.7
momentum = 0.9

tile_slots = 4
MESH = pl.DeviceIdType.MESH


def flipped(index, mask):
    bit = 1
    while bit <= mask:
        if mask & bit:
            index = index + bit * (1 - 2 * (lax.div(index, bit) % 2))
        bit *= 2
    return index


def outer_update(weight, moment, mean_direction):
    pseudo = inner_rate * (mean_direction + decay_rate * weight)
    moment_new = momentum * moment + pseudo
    return weight - outer_rate * (pseudo + momentum * moment_new), moment_new


def adam_direction(gradient, first_moment, second_moment):
    first_new = beta_first * first_moment + (1.0 - beta_first) * gradient
    second_new = beta_second * second_moment + (1.0 - beta_second) * gradient * gradient
    return (first_new * (1.0 / bias_first)) / (
        jnp.sqrt(second_new * (1.0 / bias_second)) + adam_eps
    )


def kernel(
    levels, columns, capacity,
    assign_ref, tokens_ref, level_one_ref, moment_one_ref, level_two_ref, moment_two_ref,
    first_one_ref, second_one_ref, first_two_ref, second_two_ref,
    new_one_ref, new_moment_one_ref, new_two_ref, new_moment_two_ref,
    packed, arrived, count_out, count_in, weight_one, weight_two,
    adam_one_m, adam_one_v, adam_two_m, adam_two_v, grad_one, grad_two,
    own_one, own_two, out_one, out_two, in_one, in_two,
    local_sem, piece_send, piece_recv, count_send, count_recv,
    w1_send, w1_recv, w2_send, w2_forward, w2_recv, d1_send, d1_recv, d2_send, d2_recv,
):
    row = lax.axis_index("row")
    col = lax.axis_index("col")
    number, length, features = tokens_ref.shape
    rows_one = features // columns
    rows_two = features // levels
    piece = min(capacity, tile_slots)
    own_pieces = capacity // piece
    per_tile = tile_slots // piece
    tiles = levels * capacity // tile_slots
    tile_rows = tile_slots * length
    shrink = features ** (-0.5)
    loss_scale = 1.0 / (number * length)

    barrier = pltpu.get_barrier_semaphore()
    for o in range(1, levels):
        pl.semaphore_signal(
            barrier, inc=1, device_id={"row": flipped(row, o)}, device_id_type=MESH
        )
    for o in range(1, columns):
        pl.semaphore_signal(
            barrier, inc=1, device_id={"col": (col + o) % columns}, device_id_type=MESH
        )

    loads = [
        pltpu.make_async_copy(source, target, local_sem.at[i])
        for i, (source, target) in enumerate((
            (first_one_ref, adam_one_m), (second_one_ref, adam_one_v),
            (first_two_ref, adam_two_m), (second_two_ref, adam_two_v),
        ))
    ]
    for load in loads:
        load.start()

    def shard_one(index):
        return weight_one.at[pl.ds(pl.multiple_of(index * rows_one, rows_one), rows_one)]

    def shard_two(index):
        return weight_two.at[pl.ds(pl.multiple_of(index * rows_two, rows_two), rows_two)]

    shard_one(col)[...] = level_one_ref[...].astype(jnp.bfloat16)
    shard_two(row)[...] = level_two_ref[...].astype(jnp.bfloat16)

    pl.semaphore_wait(barrier, levels - 1 + columns - 1)

    def send_one(o):
        return pltpu.make_async_remote_copy(
            src_ref=shard_one(col), dst_ref=shard_one(col),
            send_sem=w1_send.at[o], recv_sem=w1_recv.at[o],
            device_id={"col": (col + o) % columns}, device_id_type=MESH,
        )

    def send_two(o):
        return pltpu.make_async_remote_copy(
            src_ref=shard_two(row), dst_ref=shard_two(row),
            send_sem=w2_send.at[o], recv_sem=w2_recv.at[o],
            device_id={"row": flipped(row, o)}, device_id_type=MESH,
        )

    def forward_two(o):
        source = flipped(row, o)
        return pltpu.make_async_remote_copy(
            src_ref=shard_two(source), dst_ref=shard_two(source),
            send_sem=w2_forward.at[o], recv_sem=w2_recv.at[o + 1],
            device_id={"row": flipped(row, 1)}, device_id_type=MESH,
        )

    direct_two = [o for o in range(1, levels) if o == 1 or o % 2 == 0]
    for o in range(1, columns):
        send_one(o).start()
    for o in reversed(direct_two):
        send_two(o).start()

    def send_piece(o, p):
        start = (o - 1) * capacity + p * piece
        return pltpu.make_async_remote_copy(
            src_ref=packed.at[pl.ds(start * length, piece * length)],
            dst_ref=arrived.at[pl.ds((start + capacity) * length, piece * length)],
            send_sem=piece_send.at[o * own_pieces + p],
            recv_sem=piece_recv.at[o * own_pieces + p],
            device_id={"row": flipped(row, o)}, device_id_type=MESH,
        )

    def send_count(o):
        return pltpu.make_async_remote_copy(
            src_ref=count_out.at[o], dst_ref=count_in.at[o],
            send_sem=count_send.at[o], recv_sem=count_recv.at[o],
            device_id={"row": flipped(row, o)}, device_id_type=MESH,
        )

    for o in list(range(2, levels)) + [1, 0]:
        target = flipped(row, o)
        word = jnp.int32(0)
        scale = jnp.int32(1)
        count = jnp.int32(0)
        for b in range(number):
            hit = assign_ref[b] == target
            word = word + jnp.where(hit, b * scale, 0)
            scale = jnp.where(hit, scale * 16, scale)
            count = count + jnp.where(hit, 1, 0)
        if o == 0:
            count_in[0] = jnp.full((8, 128), count, jnp.int32)
        else:
            count_out[o] = jnp.full((8, 128), count, jnp.int32)
            send_count(o).start()
        for k in range(capacity):
            block = lax.shift_right_logical(word, jnp.int32(4 * k)) & 15
            value = tokens_ref[block]
            value = jnp.where(k < count, value, jnp.zeros_like(value))
            if o == 0:
                arrived[pl.ds(k * length, length)] = value
            else:
                packed[pl.ds(((o - 1) * capacity + k) * length, length)] = value
                if (k + 1) % piece == 0:
                    send_piece(o, k // piece).start()

    for o in range(2, levels, 2):
        send_two(o).wait_recv()
        forward_two(o).start()

    grad_one[...] = jnp.zeros_like(grad_one)
    grad_two[...] = jnp.zeros_like(grad_two)
    for o in range(1, levels):
        send_count(o).wait_recv()
    for o in range(1, columns):
        send_one(o).wait_recv()
    for o in range(1, levels, 2):
        send_two(o).wait_recv()

    def tile_body(t, carry):
        for i in range(per_tile):
            g = t * per_tile + i
            part = arrived.at[pl.ds(pl.multiple_of(g * piece * length, piece * length), piece * length)]

            @pl.when(g >= own_pieces)
            def _():
                pltpu.make_async_remote_copy(
                    src_ref=part, dst_ref=part,
                    send_sem=piece_send.at[g], recv_sem=piece_recv.at[g],
                    device_id={"row": flipped(row, 1)}, device_id_type=MESH,
                ).wait_recv()

        inputs = arrived[pl.ds(pl.multiple_of(t * tile_rows, tile_rows), tile_rows)].astype(jnp.float32)
        place = lax.broadcasted_iota(jnp.int32, (tile_rows, 1), 0)
        inner = place % length
        slot = t * tile_slots + place // length
        if capacity >= tile_slots:
            count = count_in[(t * tile_slots) // capacity][0:1, 0:1]
        else:
            count = jnp.zeros((1, 1), jnp.int32)
            per_source = tile_slots // capacity
            for i in range(per_source):
                own = count_in[t * per_source + i][0:1, 0:1]
                count = jnp.where(place // (capacity * length) == i, own, count)
        filled = (slot % capacity < count).astype(jnp.float32)
        loss_weight = filled * (inner < length - 1).astype(jnp.float32) * loss_scale
        targets = jnp.where(inner < length - 1, pltpu.roll(inputs, tile_rows - 1, 0), 0.0)

        factor_one = lax.rsqrt(jnp.mean(inputs * inputs, axis=-1, keepdims=True) + norm_eps)
        act_one = (inputs * factor_one).astype(jnp.bfloat16)
        pre_one = shrink * jnp.dot(act_one, weight_one[...], preferred_element_type=jnp.float32)
        gate_one = jax.nn.sigmoid(pre_one)
        hidden = inputs + pre_one * gate_one
        factor_two = lax.rsqrt(jnp.mean(hidden * hidden, axis=-1, keepdims=True) + norm_eps)
        normed_two = hidden * factor_two
        act_two = normed_two.astype(jnp.bfloat16)
        pre_two = shrink * jnp.dot(act_two, weight_two[...], preferred_element_type=jnp.float32)
        gate_two = jax.nn.sigmoid(pre_two)
        grad_out = loss_weight * (hidden + pre_two * gate_two - targets)
        grad_pre_two = (grad_out * (gate_two * (1.0 + pre_two * (1.0 - gate_two)))).astype(jnp.bfloat16)
        grad_two[...] += lax.dot_general(
            act_two, grad_pre_two, (((0,), (0,)), ((), ())), preferred_element_type=jnp.float32
        )
        grad_act = shrink * lax.dot_general(
            grad_pre_two, weight_two[...], (((1,), (1,)), ((), ())),
            preferred_element_type=jnp.float32,
        )
        grad_hidden = grad_out + factor_two * (
            grad_act - normed_two * jnp.mean(grad_act * normed_two, axis=-1, keepdims=True)
        )
        grad_pre_one = (grad_hidden * (gate_one * (1.0 + pre_one * (1.0 - gate_one)))).astype(jnp.bfloat16)
        grad_one[...] += lax.dot_general(
            act_one, grad_pre_one, (((0,), (0,)), ((), ())), preferred_element_type=jnp.float32
        )
        return carry

    lax.fori_loop(0, tiles, tile_body, 0)

    for load in loads:
        load.wait()

    def direction(grad, first, second, index, rows):
        at = pl.ds(pl.multiple_of(index * rows, rows), rows)
        return adam_direction(shrink * grad[at, :], first[at, :], second[at, :])

    def send_direction_one(o):
        return pltpu.make_async_remote_copy(
            src_ref=out_one.at[o], dst_ref=in_one.at[o],
            send_sem=d1_send.at[o], recv_sem=d1_recv.at[o],
            device_id={"col": (col + o) % columns}, device_id_type=MESH,
        )

    def send_direction_two(o):
        return pltpu.make_async_remote_copy(
            src_ref=out_two.at[o], dst_ref=in_two.at[o],
            send_sem=d2_send.at[o], recv_sem=d2_recv.at[o],
            device_id={"row": flipped(row, o)}, device_id_type=MESH,
        )

    for o in range(1, max(levels, columns)):
        if o < columns:
            out_one[o] = direction(
                grad_one, adam_one_m, adam_one_v, (col + o) % columns, rows_one
            ).astype(jnp.bfloat16)
            send_direction_one(o).start()
        if o < levels:
            q = levels - o
            out_two[q] = direction(
                grad_two, adam_two_m, adam_two_v, flipped(row, q), rows_two
            ).astype(jnp.bfloat16)
            send_direction_two(q).start()
    own_one[...] = direction(grad_one, adam_one_m, adam_one_v, col, rows_one)
    own_two[...] = direction(grad_two, adam_two_m, adam_two_v, row, rows_two)

    for o in range(1, levels):
        send_direction_two(o).wait_recv()
    total_two = own_two[...]
    for o in range(1, levels):
        total_two = total_two + in_two[o].astype(jnp.float32)
    new, moment = outer_update(level_two_ref[...], moment_two_ref[...], total_two / levels)
    new_two_ref[...] = new
    new_moment_two_ref[...] = moment

    for o in range(1, columns):
        send_direction_one(o).wait_recv()
    total_one = own_one[...]
    for o in range(1, columns):
        total_one = total_one + in_one[o].astype(jnp.float32)
    new, moment = outer_update(level_one_ref[...], moment_one_ref[...], total_one / columns)
    new_one_ref[...] = new
    new_moment_one_ref[...] = moment

    for o in range(1, columns):
        send_one(o).wait_send()
        send_direction_one(o).wait_send()
    for o in direct_two:
        send_two(o).wait_send()
    for o in range(2, levels, 2):
        forward_two(o).wait_send()
    for o in range(1, levels):
        send_count(o).wait_send()
        send_direction_two(o).wait_send()
        for p in range(own_pieces):
            send_piece(o, p).wait_send()


def per_device(
    tokens, assign, level_one, moment_one, level_two, moment_two,
    first_one, second_one, first_two, second_two,
):
    levels = lax.axis_size("row")
    columns = lax.axis_size("col")
    blocks = tokens[0, 0]
    number, length, features = blocks.shape
    capacity = max(2, (2 * number + levels - 1) // levels)
    rows_one = features // columns
    rows_two = features // levels
    piece = min(capacity, tile_slots)
    pieces = levels * capacity // piece
    f32, bf16 = jnp.float32, jnp.bfloat16
    vmem = pl.BlockSpec(memory_space=pltpu.VMEM)
    smem = pl.BlockSpec(memory_space=pltpu.SMEM)
    hbm = pl.BlockSpec(memory_space=pl.ANY)
    dma = pltpu.SemaphoreType.DMA
    square = (features, features)
    outs = pl.pallas_call(
        functools.partial(kernel, levels, columns, capacity),
        out_shape=[
            jax.ShapeDtypeStruct((rows_one, features), f32),
            jax.ShapeDtypeStruct((rows_one, features), f32),
            jax.ShapeDtypeStruct((rows_two, features), f32),
            jax.ShapeDtypeStruct((rows_two, features), f32),
        ],
        in_specs=[smem] + [vmem] * 5 + [hbm] * 4,
        out_specs=[vmem] * 4,
        scratch_shapes=[
            pltpu.VMEM(((levels - 1) * capacity * length, features), bf16),
            pltpu.VMEM((levels * capacity * length, features), bf16),
            pltpu.VMEM((levels, 8, 128), jnp.int32),
            pltpu.VMEM((levels, 8, 128), jnp.int32),
            pltpu.VMEM(square, bf16),
            pltpu.VMEM(square, bf16),
            pltpu.VMEM(square, f32),
            pltpu.VMEM(square, f32),
            pltpu.VMEM(square, f32),
            pltpu.VMEM(square, f32),
            pltpu.VMEM(square, f32),
            pltpu.VMEM(square, f32),
            pltpu.VMEM((rows_one, features), f32),
            pltpu.VMEM((rows_two, features), f32),
            pltpu.VMEM((columns, rows_one, features), bf16),
            pltpu.VMEM((levels, rows_two, features), bf16),
            pltpu.VMEM((columns, rows_one, features), bf16),
            pltpu.VMEM((levels, rows_two, features), bf16),
            dma((4,)),
            dma((pieces,)), dma((pieces,)),
            dma((levels,)), dma((levels,)),
            dma((columns,)), dma((columns,)),
            dma((levels,)), dma((levels,)), dma((levels,)),
            dma((columns,)), dma((columns,)),
            dma((levels,)), dma((levels,)),
        ],
        compiler_params=pltpu.CompilerParams(
            collective_id=0, has_side_effects=True, vmem_limit_bytes=56 * 1024 * 1024
        ),
        name="outer_round",
    )(
        assign.reshape(number), blocks, level_one[0], moment_one[0], level_two[0], moment_two[0],
        first_one[0, 0], second_one[0, 0], first_two[0, 0], second_two[0, 0],
    )
    return tuple(out[None] for out in outs)


def solution(mesh):
    in_specs = (
        P(("groups", "row"), "col", None, None, None),
        P(("groups", "row"), "col", None, None),
        P(("groups", "row"), "col", None),
        P(("groups", "row"), "col", None),
        P(("groups", "col"), "row", None),
        P(("groups", "col"), "row", None),
        P(("groups", "row"), "col", None, None),
        P(("groups", "row"), "col", None, None),
        P(("groups", "row"), "col", None, None),
        P(("groups", "row"), "col", None, None),
    )
    out_specs = (
        P(("groups", "row"), "col", None),
        P(("groups", "row"), "col", None),
        P(("groups", "col"), "row", None),
        P(("groups", "col"), "row", None),
    )
    return jax.shard_map(
        per_device, mesh=mesh, in_specs=in_specs, out_specs=out_specs, check_vma=False
    )
```

time: 279 us -> 90.9 us (0.33)
  the two profiles are of different devices: /device:TPU:0 before, /device:TPU:28 now
where the time goes in v1:
time: 90.9 us; the launch traced here: 90.7 us
  Pallas kernels  84.5 us (93%)
  local copies, waits for them, and re-layouts  5.56 us (6%)
    pallas_call x1, Pallas kernels, per_device(): pl.pallas_call(functools.partial(kernel, levels, columns, capacity), out_...  84.5 us
    unnamed x8, local copies, waits for them, and re-layouts  5.56 us

profile of v1, /device:TPU:28, one launch (start us, length us, event | category | flops | bytes accessed | tf_op | source)
XLA Modules:
  0.0 90.7 jit_solution(10237147998450171948)
XLA Ops:
  0.6 84.5 %outer_round.1 = (f32[192,768]{1,0:T(8,128)}, f32[192,768]{1,0:T(8,128)}, f32[192,768]{1,0:T(8,128)}, f32[192,768]{1,0:T(8,128)}) custom-call(s32[16]{0:T(128)} %bitcast.27, bf16[16,64,768]{2,1,0:T(8,128)(2,1)} %bitcast.18, f32[192,768]{1,0:T(8,128)} %bitcast.23, f32[192,768]{1,0:T(8,128)} %bitcast.24, f32[192,768]{1,0:T(8,128)} %bitcast.25, ...), custom_call_target="tpu_custom_call" | custom-call | tf_op jit(solution)/shard_map/outer_round/pallas_call | solution.py:333
  85.1 0.0 copy-start.1
  85.1 0.0 copy-start
  85.1 2.0 %copy.18 = f32[1,192,768]{2,1,0:T(8,128)} copy(f32[1,192,768]{2,1,0:T(8,128)} %bitcast.22) | data formatting | bytes 1179648
  87.1 1.9 %copy.19 = f32[1,192,768]{2,1,0:T(8,128)} copy(f32[1,192,768]{2,1,0:T(8,128)} %bitcast.21) | data formatting | bytes 1179648
  89.0 0.0 copy-done.1
  89.0 0.8 copy.20
  89.9 0.0 copy-done
  89.9 0.8 copy.21
Async XLA Ops:
  85.1 3.9 %copy-start.1 = (f32[192,768]{1,0:T(8,128)S(1)}, f32[192,768]{1,0:T(8,128)}, u32[]{:S(2)}) copy-start(f32[192,768]{1,0:T(8,128)} %get-tuple-element.10) | copy-start | bytes 1769476
  85.1 4.8 %copy-start = (f32[192,768]{1,0:T(8,128)S(1)}, f32[192,768]{1,0:T(8,128)}, u32[]{:S(2)}) copy-start(f32[192,768]{1,0:T(8,128)} %get-tuple-element.11) | copy-start | bytes 1769476

commit v2 on v1

--- a/solution.py
+++ b/solution.py
@@ -47,14 +47,15 @@
 
 def kernel(
     levels, columns, capacity,
-    assign_ref, tokens_ref, level_one_ref, moment_one_ref, level_two_ref, moment_two_ref,
+    assign_ref, tokens_hbm, level_one_hbm, level_two_hbm,
     first_one_ref, second_one_ref, first_two_ref, second_two_ref,
-    new_one_ref, new_moment_one_ref, new_two_ref, new_moment_two_ref,
-    packed, arrived, count_out, count_in, weight_one, weight_two,
+    mean_one_ref, mean_two_ref,
+    tokens_ref, level_one_ref, level_two_ref, relay_in, relay_out, packed, arrived, count_out, count_in, weight_one, weight_two,
     adam_one_m, adam_one_v, adam_two_m, adam_two_v, grad_one, grad_two,
     own_one, own_two, out_one, out_two, in_one, in_two,
     local_sem, piece_send, piece_recv, count_send, count_recv,
     w1_send, w1_recv, w2_send, w2_forward, w2_recv, d1_send, d1_recv, d2_send, d2_recv,
+    relay_send, relay_recv,
 ):
     row = lax.axis_index("row")
     col = lax.axis_index("col")
@@ -86,7 +87,13 @@
             (first_two_ref, adam_two_m), (second_two_ref, adam_two_v),
         ))
     ]
-    for load in loads:
+    inputs_in = [
+        pltpu.make_async_copy(source, target, local_sem.at[4 + i])
+        for i, (source, target) in enumerate((
+            (level_two_hbm, level_two_ref), (tokens_hbm, tokens_ref), (level_one_hbm, level_one_ref),
+        ))
+    ]
+    for load in inputs_in:
         load.start()
 
     def shard_one(index):
@@ -94,11 +101,6 @@
 
     def shard_two(index):
         return weight_two.at[pl.ds(pl.multiple_of(index * rows_two, rows_two), rows_two)]
-
-    shard_one(col)[...] = level_one_ref[...].astype(jnp.bfloat16)
-    shard_two(row)[...] = level_two_ref[...].astype(jnp.bfloat16)
-
-    pl.semaphore_wait(barrier, levels - 1 + columns - 1)
 
     def send_one(o):
         return pltpu.make_async_remote_copy(
@@ -123,11 +125,6 @@
         )
 
     direct_two = [o for o in range(1, levels) if o == 1 or o % 2 == 0]
-    for o in range(1, columns):
-        send_one(o).start()
-    for o in reversed(direct_two):
-        send_two(o).start()
-
     def send_piece(o, p):
         start = (o - 1) * capacity + p * piece
         return pltpu.make_async_remote_copy(
@@ -145,7 +142,7 @@
             device_id={"row": flipped(row, o)}, device_id_type=MESH,
         )
 
-    for o in list(range(2, levels)) + [1, 0]:
+    def pack(o):
         target = flipped(row, o)
         word = jnp.int32(0)
         scale = jnp.int32(1)
@@ -155,11 +152,8 @@
             word = word + jnp.where(hit, b * scale, 0)
             scale = jnp.where(hit, scale * 16, scale)
             count = count + jnp.where(hit, 1, 0)
-        if o == 0:
-            count_in[0] = jnp.full((8, 128), count, jnp.int32)
-        else:
-            count_out[o] = jnp.full((8, 128), count, jnp.int32)
-            send_count(o).start()
+        counts = count_in if o == 0 else count_out
+        counts[o] = jnp.full((8, 128), count, jnp.int32)
         for k in range(capacity):
             block = lax.shift_right_logical(word, jnp.int32(4 * k)) & 15
             value = tokens_ref[block]
@@ -168,12 +162,45 @@
                 arrived[pl.ds(k * length, length)] = value
             else:
                 packed[pl.ds(((o - 1) * capacity + k) * length, length)] = value
-                if (k + 1) % piece == 0:
-                    send_piece(o, k // piece).start()
-
+
+    inputs_in[0].wait()
+    direct_two = [o for o in range(1, levels) if o == 1 or o % 2 == 0]
+    shard_two(row)[...] = level_two_ref[...].astype(jnp.bfloat16)
+    inputs_in[1].wait()
+    pack(2)
+    inputs_in[2].wait()
+    shard_one(col)[...] = level_one_ref[...].astype(jnp.bfloat16)
+
+    pl.semaphore_wait(barrier, levels - 1 + columns - 1)
+
+    far = [(o, p) for o in range(2, levels) for p in range(own_pieces)]
+    for o in reversed(direct_two):
+        send_two(o).start()
+    send_piece(*far[0]).start()
+    for o in range(1, columns):
+        send_one(o).start()
+    send_count(2).start()
+    pack(1)
+    send_count(1).start()
+    for p in range(own_pieces):
+        send_piece(1, p).start()
+    for o in range(3, levels):
+        pack(o)
+        send_count(o).start()
+    pack(0)
+    for load in loads:
+        load.start()
+
+    for o in direct_two:
+        if o > 1:
+            send_two(o).wait_send()
+    send_piece(*far[1]).start()
     for o in range(2, levels, 2):
         send_two(o).wait_recv()
         forward_two(o).start()
+    for i in range(2, len(far) - 1):
+        send_piece(*far[i - 2]).wait_send()
+        send_piece(*far[i]).start()
 
     grad_one[...] = jnp.zeros_like(grad_one)
     grad_two[...] = jnp.zeros_like(grad_two)
@@ -241,7 +268,11 @@
         )
         return carry
 
-    lax.fori_loop(0, tiles, tile_body, 0)
+    first_tiles = max(1, own_pieces // per_tile)
+    lax.fori_loop(0, first_tiles, tile_body, 0)
+    send_piece(*far[-3]).wait_send()
+    send_piece(*far[-1]).start()
+    lax.fori_loop(first_tiles, tiles, tile_body, 0)
 
     for load in loads:
         load.wait()
@@ -264,19 +295,68 @@
             device_id={"row": flipped(row, o)}, device_id_type=MESH,
         )
 
-    for o in range(1, max(levels, columns)):
-        if o < columns:
-            out_one[o] = direction(
-                grad_one, adam_one_m, adam_one_v, (col + o) % columns, rows_one
-            ).astype(jnp.bfloat16)
-            send_direction_one(o).start()
-        if o < levels:
-            q = levels - o
-            out_two[q] = direction(
-                grad_two, adam_two_m, adam_two_v, flipped(row, q), rows_two
-            ).astype(jnp.bfloat16)
-            send_direction_two(q).start()
-    own_one[...] = direction(grad_one, adam_one_m, adam_one_v, col, rows_one)
+    def relay(target):
+        return pltpu.make_async_remote_copy(
+            src_ref=relay_out, dst_ref=relay_in, send_sem=relay_send, recv_sem=relay_recv,
+            device_id={"col": target}, device_id_type=MESH,
+        )
+
+    def one_for(index):
+        return direction(grad_one, adam_one_m, adam_one_v, index, rows_one)
+
+    def start_one(o):
+        out_one[o] = one_for((col + o) % columns).astype(jnp.bfloat16)
+        send_direction_one(o).start()
+
+    def start_two(o):
+        out_two[o] = direction(
+            grad_two, adam_two_m, adam_two_v, flipped(row, o), rows_two
+        ).astype(jnp.bfloat16)
+        send_direction_two(o).start()
+
+    line = columns == 4
+    if line:
+        at_end = lax.rem(col, 3) == 0
+
+        @pl.when(at_end)
+        def _():
+            relay_out[...] = one_for(3 - col).astype(jnp.bfloat16)
+
+        @pl.when(col == 0)
+        def _():
+            relay(1).start()
+            start_one(2)
+            start_one(1)
+
+        @pl.when(col == 3)
+        def _():
+            relay(2).start()
+            start_one(2)
+            start_one(3)
+
+        @pl.when(col == 1)
+        def _():
+            start_one(3)
+            start_one(1)
+
+        @pl.when(col == 2)
+        def _():
+            start_one(1)
+            start_one(3)
+    else:
+        for o in range(1, columns):
+            start_one(o)
+    for o in range(levels - 1, 0, -1):
+        start_two(o)
+    if line:
+        @pl.when(jnp.logical_not(at_end))
+        def _():
+            own_one[...] = one_for(3 * (2 - col))
+            relay(3 * (2 - col)).wait_recv()
+            out_one[2] = (own_one[...] + relay_in[...].astype(jnp.float32)).astype(jnp.bfloat16)
+            send_direction_one(2).start()
+
+    own_one[...] = one_for(col)
     own_two[...] = direction(grad_two, adam_two_m, adam_two_v, row, rows_two)
 
     for o in range(1, levels):
@@ -284,31 +364,46 @@
     total_two = own_two[...]
     for o in range(1, levels):
         total_two = total_two + in_two[o].astype(jnp.float32)
-    new, moment = outer_update(level_two_ref[...], moment_two_ref[...], total_two / levels)
-    new_two_ref[...] = new
-    new_moment_two_ref[...] = moment
-
-    for o in range(1, columns):
-        send_direction_one(o).wait_recv()
-    total_one = own_one[...]
-    for o in range(1, columns):
-        total_one = total_one + in_one[o].astype(jnp.float32)
-    new, moment = outer_update(level_one_ref[...], moment_one_ref[...], total_one / columns)
-    new_one_ref[...] = new
-    new_moment_one_ref[...] = moment
+    mean_two_ref[...] = total_two / levels
+
+    def receive_one(sent, offsets):
+        for o in offsets:
+            send_direction_one(o).wait_recv()
+        total_one = own_one[...]
+        for o in offsets:
+            total_one = total_one + in_one[o].astype(jnp.float32)
+        mean_one_ref[...] = total_one / columns
+        for o in sent:
+            send_direction_one(o).wait_send()
+
+    if line:
+        @pl.when(col == 0)
+        def _():
+            receive_one((1, 2), (3, 2))
+            relay(1).wait_send()
+
+        @pl.when(col == 3)
+        def _():
+            receive_one((2, 3), (1, 2))
+            relay(2).wait_send()
+
+        @pl.when(jnp.logical_not(at_end))
+        def _():
+            receive_one((1, 2, 3), (1, 3, 2))
+    else:
+        receive_one(range(1, columns), range(1, columns))
 
     for o in range(1, columns):
         send_one(o).wait_send()
-        send_direction_one(o).wait_send()
-    for o in direct_two:
-        send_two(o).wait_send()
+    send_two(1).wait_send()
     for o in range(2, levels, 2):
         forward_two(o).wait_send()
     for o in range(1, levels):
         send_count(o).wait_send()
         send_direction_two(o).wait_send()
         for p in range(own_pieces):
-            send_piece(o, p).wait_send()
+            if o == 1 or (o, p) in far[-2:]:
+                send_piece(o, p).wait_send()
 
 
 def per_device(
@@ -327,20 +422,23 @@
     f32, bf16 = jnp.float32, jnp.bfloat16
     vmem = pl.BlockSpec(memory_space=pltpu.VMEM)
     smem = pl.BlockSpec(memory_space=pltpu.SMEM)
-    hbm = pl.BlockSpec(memory_space=pl.ANY)
+    hbm = pl.BlockSpec(memory_space=pltpu.HBM)
     dma = pltpu.SemaphoreType.DMA
     square = (features, features)
-    outs = pl.pallas_call(
+    mean_one, mean_two = pl.pallas_call(
         functools.partial(kernel, levels, columns, capacity),
         out_shape=[
             jax.ShapeDtypeStruct((rows_one, features), f32),
-            jax.ShapeDtypeStruct((rows_one, features), f32),
-            jax.ShapeDtypeStruct((rows_two, features), f32),
             jax.ShapeDtypeStruct((rows_two, features), f32),
         ],
-        in_specs=[smem] + [vmem] * 5 + [hbm] * 4,
-        out_specs=[vmem] * 4,
+        in_specs=[smem] + [hbm] * 7,
+        out_specs=[vmem] * 2,
         scratch_shapes=[
+            pltpu.VMEM((number, length, features), bf16),
+            pltpu.VMEM((rows_one, features), f32),
+            pltpu.VMEM((rows_two, features), f32),
+            pltpu.VMEM((rows_one, features), bf16),
+            pltpu.VMEM((rows_one, features), bf16),
             pltpu.VMEM(((levels - 1) * capacity * length, features), bf16),
             pltpu.VMEM((levels * capacity * length, features), bf16),
             pltpu.VMEM((levels, 8, 128), jnp.int32),
@@ -359,23 +457,26 @@
             pltpu.VMEM((levels, rows_two, features), bf16),
             pltpu.VMEM((columns, rows_one, features), bf16),
             pltpu.VMEM((levels, rows_two, features), bf16),
-            dma((4,)),
+            dma((7,)),
             dma((pieces,)), dma((pieces,)),
             dma((levels,)), dma((levels,)),
             dma((columns,)), dma((columns,)),
             dma((levels,)), dma((levels,)), dma((levels,)),
             dma((columns,)), dma((columns,)),
             dma((levels,)), dma((levels,)),
+            dma, dma,
         ],
         compiler_params=pltpu.CompilerParams(
             collective_id=0, has_side_effects=True, vmem_limit_bytes=56 * 1024 * 1024
         ),
         name="outer_round",
     )(
-        assign.reshape(number), blocks, level_one[0], moment_one[0], level_two[0], moment_two[0],
+        assign.reshape(number), blocks, level_one[0], level_two[0],
         first_one[0, 0], second_one[0, 0], first_two[0, 0], second_two[0, 0],
     )
-    return tuple(out[None] for out in outs)
+    new_one, new_moment_one = outer_update(level_one[0], moment_one[0], mean_one)
+    new_two, new_moment_two = outer_update(level_two[0], moment_two[0], mean_two)
+    return (new_one[None], new_moment_one[None], new_two[None], new_moment_two[None])
 
 
 def solution(mesh):

time: 90.9 us -> 82.2 us (0.904)
  the two profiles are of different devices: /device:TPU:28 before, /device:TPU:0 now
where the time goes in v2:
time: 82.2 us; the launch traced here: 82 us
  Pallas kernels  78.5 us (95%)
  other arithmetic  2.84 us (3%)
    pallas_call x1, Pallas kernels, per_device(): pl.pallas_call(functools.partial(kernel, levels, columns, capacity), out_...  78.5 us
    broadcast_in_dim x1, other arithmetic, per_device(): new_moment_one[None]  2.84 us

profile of v2, /device:TPU:0, one launch (start us, length us, event | category | flops | bytes accessed | tf_op | source)
XLA Modules:
  0.0 82.0 jit_solution(4093755260288592045)
XLA Ops:
  0.6 0.0 copy-start
  0.6 0.0 copy-start.1
  0.7 0.0 copy-start.2
  0.7 0.0 copy-start.3
  0.7 78.5 %outer_round.1 = (f32[192,768]{1,0:T(8,128)}, f32[192,768]{1,0:T(8,128)}) custom-call(s32[16]{0:T(128)} %bitcast.39, bf16[16,64,768]{2,1,0:T(8,128)(2,1)} %bitcast.38, f32[192,768]{1,0:T(8,128)} %bitcast.32, f32[192,768]{1,0:T(8,128)} %bitcast.33, f32[768,768]{1,0:T(8,128)} %bitcast.34, f32[768,768]{1,0:T(8,128)} %bitcast.35, f32[768,768]{1,0:T(8,128)} %bitcast.36, ...), custom_call_target="tpu_custom_call" | custom-call | tf_op jit(solution)/shard_map/outer_round/pallas_call | solution.py:428
  79.1 0.0 copy-done
  79.2 0.0 copy-done.1
  79.2 0.0 copy-done.2
  79.2 0.0 copy-done.3
  79.2 2.8 %fusion = (f32[1,192,768]{2,1,0:T(8,128)}, f32[1,192,768]{2,1,0:T(8,128)}, f32[1,192,768]{2,1,0:T(8,128)}, f32[1,192,768]{2,1,0:T(8,128)}) fusion(f32[1,192,768]{2,1,0:T(8,128)S(1)} %copy-done.2, f32[192,768]{1,0:T(8,128)} %get-tuple-element.6, f32[1,192,768]{2,1,0:T(8,128)S(1)} %copy-done, f32[1,192,768]{2,1,0:T(8,128)S(1)} %copy-done.3, ...), kind=kLoop, calls=%fused_computation.6 | loop fusion | flops 2654208 | bytes 5898240 | tf_op jit(solution)/shard_map/broadcast_in_dim | solution.py:479
Async XLA Ops:
  0.6 78.5 %copy-start = (f32[1,192,768]{2,1,0:T(8,128)S(1)}, f32[1,192,768]{2,1,0:T(8,128)}, u32[]{:S(2)}) copy-start(f32[1,192,768]{2,1,0:T(8,128)} %param.12) | copy-start | bytes 1769476
  0.6 78.5 %copy-start.1 = (f32[1,192,768]{2,1,0:T(8,128)S(1)}, f32[1,192,768]{2,1,0:T(8,128)}, u32[]{:S(2)}) copy-start(f32[1,192,768]{2,1,0:T(8,128)} %param.14) | copy-start | bytes 1769476
  0.7 78.5 %copy-start.2 = (f32[1,192,768]{2,1,0:T(8,128)S(1)}, f32[1,192,768]{2,1,0:T(8,128)}, u32[]{:S(2)}) copy-start(f32[1,192,768]{2,1,0:T(8,128)} %param.13) | copy-start | bytes 1769476
  0.7 78.5 %copy-start.3 = (f32[1,192,768]{2,1,0:T(8,128)S(1)}, f32[1,192,768]{2,1,0:T(8,128)}, u32[]{:S(2)}) copy-start(f32[1,192,768]{2,1,0:T(8,128)} %param.15) | copy-start | bytes 1769476

commit v3 on v2

--- a/solution.py
+++ b/solution.py
@@ -18,7 +18,7 @@
 outer_rate = 0.7
 momentum = 0.9
 
-tile_slots = 4
+tile_slots = 8
 MESH = pl.DeviceIdType.MESH
 
 
@@ -173,10 +173,10 @@
 
     pl.semaphore_wait(barrier, levels - 1 + columns - 1)
 
-    far = [(o, p) for o in range(2, levels) for p in range(own_pieces)]
     for o in reversed(direct_two):
         send_two(o).start()
-    send_piece(*far[0]).start()
+    for p in range(own_pieces):
+        send_piece(2, p).start()
     for o in range(1, columns):
         send_one(o).start()
     send_count(2).start()
@@ -187,6 +187,8 @@
     for o in range(3, levels):
         pack(o)
         send_count(o).start()
+        for p in range(own_pieces):
+            send_piece(o, p).start()
     pack(0)
     for load in loads:
         load.start()
@@ -194,13 +196,9 @@
     for o in direct_two:
         if o > 1:
             send_two(o).wait_send()
-    send_piece(*far[1]).start()
     for o in range(2, levels, 2):
         send_two(o).wait_recv()
         forward_two(o).start()
-    for i in range(2, len(far) - 1):
-        send_piece(*far[i - 2]).wait_send()
-        send_piece(*far[i]).start()
 
     grad_one[...] = jnp.zeros_like(grad_one)
     grad_two[...] = jnp.zeros_like(grad_two)
@@ -268,11 +266,7 @@
         )
         return carry
 
-    first_tiles = max(1, own_pieces // per_tile)
-    lax.fori_loop(0, first_tiles, tile_body, 0)
-    send_piece(*far[-3]).wait_send()
-    send_piece(*far[-1]).start()
-    lax.fori_loop(first_tiles, tiles, tile_body, 0)
+    lax.fori_loop(0, tiles, tile_body, 0)
 
     for load in loads:
         load.wait()
@@ -402,8 +396,7 @@
         send_count(o).wait_send()
         send_direction_two(o).wait_send()
         for p in range(own_pieces):
-            if o == 1 or (o, p) in far[-2:]:
-                send_piece(o, p).wait_send()
+            send_piece(o, p).wait_send()
 
 
 def per_device(

time: 82.2 us -> 81.5 us (level)
  no operation moved by 1% of the time
where the time goes in v3:
time: 81.5 us; the launch traced here: 81.3 us
  Pallas kernels  77.8 us (95%)
  other arithmetic  2.84 us (3%)
    pallas_call x1, Pallas kernels, per_device(): pl.pallas_call(functools.partial(kernel, levels, columns, capacity), out_...  77.8 us
    broadcast_in_dim x1, other arithmetic, per_device(): new_moment_one[None]  2.84 us

profile of v3, /device:TPU:0, one launch (start us, length us, event | category | flops | bytes accessed | tf_op | source)
XLA Modules:
  0.0 81.3 jit_solution(15483366955628914411)
XLA Ops:
  0.6 0.0 copy-start
  0.6 0.0 copy-start.1
  0.7 0.0 copy-start.2
  0.7 0.0 copy-start.3
  0.7 77.8 %outer_round.1 = (f32[192,768]{1,0:T(8,128)}, f32[192,768]{1,0:T(8,128)}) custom-call(s32[16]{0:T(128)} %bitcast.39, bf16[16,64,768]{2,1,0:T(8,128)(2,1)} %bitcast.38, f32[192,768]{1,0:T(8,128)} %bitcast.32, f32[192,768]{1,0:T(8,128)} %bitcast.33, f32[768,768]{1,0:T(8,128)} %bitcast.34, f32[768,768]{1,0:T(8,128)} %bitcast.35, f32[768,768]{1,0:T(8,128)} %bitcast.36, ...), custom_call_target="tpu_custom_call" | custom-call | tf_op jit(solution)/shard_map/outer_round/pallas_call | solution.py:421
  78.4 0.0 copy-done
  78.5 0.0 copy-done.1
  78.5 0.0 copy-done.2
  78.5 0.0 copy-done.3
  78.5 2.8 %fusion = (f32[1,192,768]{2,1,0:T(8,128)}, f32[1,192,768]{2,1,0:T(8,128)}, f32[1,192,768]{2,1,0:T(8,128)}, f32[1,192,768]{2,1,0:T(8,128)}) fusion(f32[1,192,768]{2,1,0:T(8,128)S(1)} %copy-done.2, f32[192,768]{1,0:T(8,128)} %get-tuple-element.6, f32[1,192,768]{2,1,0:T(8,128)S(1)} %copy-done, f32[1,192,768]{2,1,0:T(8,128)S(1)} %copy-done.3, ...), kind=kLoop, calls=%fused_computation.6 | loop fusion | flops 2654208 | bytes 5898240 | tf_op jit(solution)/shard_map/broadcast_in_dim | solution.py:472
Async XLA Ops:
  0.6 77.8 %copy-start = (f32[1,192,768]{2,1,0:T(8,128)S(1)}, f32[1,192,768]{2,1,0:T(8,128)}, u32[]{:S(2)}) copy-start(f32[1,192,768]{2,1,0:T(8,128)} %param.12) | copy-start | bytes 1769476
  0.6 77.8 %copy-start.1 = (f32[1,192,768]{2,1,0:T(8,128)S(1)}, f32[1,192,768]{2,1,0:T(8,128)}, u32[]{:S(2)}) copy-start(f32[1,192,768]{2,1,0:T(8,128)} %param.14) | copy-start | bytes 1769476
  0.7 77.8 %copy-start.2 = (f32[1,192,768]{2,1,0:T(8,128)S(1)}, f32[1,192,768]{2,1,0:T(8,128)}, u32[]{:S(2)}) copy-start(f32[1,192,768]{2,1,0:T(8,128)} %param.13) | copy-start | bytes 1769476
  0.7 77.8 %copy-start.3 = (f32[1,192,768]{2,1,0:T(8,128)S(1)}, f32[1,192,768]{2,1,0:T(8,128)}, u32[]{:S(2)}) copy-start(f32[1,192,768]{2,1,0:T(8,128)} %param.15) | copy-start | bytes 1769476
